TPU v7x, 32 devices: a whole 2x2x4 slice. The times are simulated.
32 devices in a mesh: win: 2 (over y), pair: 4 (over z), stk: 2 (over x), lag: 2 (over core).
Axes of the slice: x: 2, y: 2, z: 4, core: 2. Of those that a mesh axis runs over, the one named last changes fastest.
Arguments:
- spectra: bfloat16 [32, 4, 256, 1024], P('win', 'pair', 'stk'), parts along dimension 0, may hold values from -40 to 40
- pair_blocks: int32 [8, 40, 2], P('win'), parts along dimension 0, may hold values from 0 to 63, as said below
- live_pairs: int32 [8], P('win'), parts along dimension 0, may hold values from 10 to 40, as said below
- stack_group: int32 [8, 40], P('win'), parts along dimension 0, may hold values from 0 to 3, as said below
Outputs:
- stacks: float32 [8, 256, 1024], P('win', 'stk', ('pair', 'lag')), parts along dimension 0
There are 2 independent parts, one for each index of `win`. A program takes and returns all parts, laid end to end along the dimension named above; each array names one. Nothing has to cross between parts.
Inputs may be any that keep to these rules, and one draw needn't show every extreme that they name: `pair_blocks`: every pair names a first block and a second block 1 to 8 higher. The pairs of all 40 slots of one owner span exactly 32 consecutive blocks, from the smallest first block to the largest second block. An owner's first live_pairs slots are used, the rest are not. Some owner uses all 40. `stack_group`: in the first 4 slots of every owner each group stands once.
All inputs are finite; a program needn't handle non-finite values.
Results may differ from a plain program's by a relative error of at most 0.0058.
Values may be sent and summed in bfloat16 or wider, within the bound.
A program may use at most 128 MiB of HBM per device.

v0:
```python
import functools
import math

import jax
import jax.numpy as jnp
import numpy as np
from jax import lax
from jax.experimental import pallas as pl
from jax.experimental.pallas import tpu as pltpu
from jax.sharding import PartitionSpec as P

NGRP = 4
HW = 15
AMP_FLOOR = 0.5
EPSILON = 1e-06
ROWS = 16
BATCH = 16
QUAD = 4
CHUNKS = 4
COLS = 128
CHUNK_ROWS = 4
PARTS = 2


def tables(num_bins):
    bins = np.arange(num_bins)[:, None]
    steps = np.arange(num_bins)[None, :]
    angles = (bins * steps % (2 * num_bins)) * (math.pi / num_bins)
    scale = math.sqrt(2.0 / num_bins)
    cosine = np.cos(angles) * scale
    sine = np.sin(angles) * scale
    upper = np.concatenate([cosine, sine], axis=1)
    lower = np.concatenate([-sine, cosine], axis=1)
    even = np.concatenate([upper[0::2], lower[0::2]], axis=0)
    odd = np.concatenate([upper[1::2], lower[1::2]], axis=0)
    shape = (num_bins, 2, num_bins // COLS, COLS)
    even, odd = (t.reshape(shape).swapaxes(1, 2).reshape(t.shape) for t in (even, odd))
    return tuple(jnp.asarray(t, jnp.bfloat16) for t in (even, odd))


def bin_order(bins):
    row = lax.broadcasted_iota(jnp.int32, (bins, bins), 0)
    col = lax.broadcasted_iota(jnp.int32, (bins, bins), 1)
    place = jnp.where(col < bins // 2, 2 * col, 2 * col - (bins - 1))
    return jnp.where(row == place, 1.0, 0.0).astype(jnp.bfloat16)


def kernel(
    pairs, live, groups, white, even_ref, odd_ref, out_ref,
    cross, acc, first_ids, second_ids, quad_at, quad_group, counts,
):
    owners = live.shape[0]
    blocks, (_, rows, width) = white.shape[0] - 1, white.shape
    bins = width // 2
    half = bins // 2

    stride = (first_ids.shape[0] - QUAD) // NGRP

    def add_owner(q, carry):
        def add_slot(s, carry):
            group = groups[q, s]
            count = counts[group]
            at = group * stride + count
            first_ids[at] = pairs[q, 0, s]
            second_ids[at] = pairs[q, 1, s]
            counts[group] = count + 1
            return carry

        return lax.fori_loop(0, live[q], add_slot, carry)

    for g in range(NGRP):
        counts[g] = 0
    lax.fori_loop(0, owners, add_owner, 0)

    def blank(at):
        for i in range(QUAD):
            first_ids[at + i] = blocks
            second_ids[at + i] = blocks

    total = 0
    for g in range(NGRP):
        blank(g * stride + counts[g])

        def add_quad(n, total, g=g):
            quad_at[total] = g * stride + n * QUAD
            quad_group[total] = g
            return total + 1

        total = lax.fori_loop(0, pl.cdiv(counts[g], QUAD), add_quad, total)
    blank(NGRP * stride)
    for i in range(BATCH // QUAD):
        quad_at[total + i] = NGRP * stride
        quad_group[total + i] = 0

    acc[...] = jnp.zeros_like(acc)

    def add_batch(step, carry):
        base = step * (BATCH // QUAD)
        for i in range(BATCH):
            at = quad_at[base + i // QUAD] + i % QUAD
            first = white[first_ids[at]].astype(jnp.float32)
            second = white[second_ids[at]].astype(jnp.float32)
            for n in range(2):
                lo, mid, hi = 2 * n * half, (2 * n + 1) * half, (2 * n + 2) * half
                ra, ia = first[:, lo:mid], first[:, mid:hi]
                rb, ib = second[:, lo:mid], second[:, mid:hi]
                cross[i * rows : (i + 1) * rows, lo:mid] = (ra * rb + ia * ib).astype(jnp.bfloat16)
                cross[i * rows : (i + 1) * rows, mid:hi] = (ia * rb - ra * ib).astype(jnp.bfloat16)
        for col in range(0, bins, COLS):
            def product(n, table):
                both = jnp.dot(
                    cross[:, n * bins : (n + 1) * bins],
                    table[:, 2 * col : 2 * (col + COLS)],
                    preferred_element_type=jnp.float32,
                )
                return both[:, :COLS], both[:, COLS:]

            even_d, even_q = product(0, even_ref)
            odd_d, odd_q = product(1, odd_ref)
            for u in range(BATCH // QUAD):
                start = pl.multiple_of(quad_group[base + u] * rows, rows)
                for side, at in ((-1, col), (1, bins + col)):
                    sums = [0.0, 0.0, 0.0]
                    for i in range(u * QUAD, (u + 1) * QUAD):
                        cut = slice(i * rows, (i + 1) * rows)
                        if side < 0:
                            direct, quad = even_d[cut] - odd_d[cut], even_q[cut] - odd_q[cut]
                        else:
                            direct, quad = even_d[cut] + odd_d[cut], even_q[cut] + odd_q[cut]
                        inverse = jnp.minimum(
                            lax.rsqrt(direct * direct + quad * quad), 1.0 / AMP_FLOOR
                        )
                        terms = (direct, direct * inverse, quad * inverse)
                        sums = [x + y for x, y in zip(sums, terms)]
                    for n, term in enumerate(sums):
                        acc[n, pl.ds(start, rows), at : at + COLS] += term
        return carry

    lax.fori_loop(0, pl.cdiv(total, BATCH // QUAD), add_batch, 0)

    pad = 128
    lags = 2 * bins
    span = lags + pad
    for g in range(NGRP):
        cut = slice(g * rows, (g + 1) * rows)
        root = jnp.sqrt(jnp.full((rows, lags), counts[g].astype(jnp.float32)))
        cosine, sine = acc[1, cut], acc[2, cut]
        coherence = jnp.sqrt(cosine * cosine + sine * sine) / root
        padded = jnp.concatenate([coherence, jnp.zeros((rows, pad), jnp.float32)], axis=1)
        part, smooth, at = padded, padded, 1
        for n in range(1, 5):
            part = part + pltpu.roll(part, span - (1 << (n - 1)), 1)
            smooth = smooth + pltpu.roll(part, span - at, 1)
            at += 1 << n
        smooth = pltpu.roll(smooth, HW, 1)[:, :lags] / (2 * HW + 1)
        out_ref[g] = ((acc[0, cut] / root) * smooth * smooth).astype(out_ref.dtype)


def whiten(values, order):
    bins = values.shape[1] // 2
    half = bins // 2
    values = values.astype(jnp.float32)
    power = jnp.sum(values * values, axis=-1, keepdims=True) * (1.0 / bins)
    whitened = (values / jnp.sqrt(power + EPSILON)).astype(jnp.bfloat16)
    real = jnp.dot(whitened[:, :bins], order, preferred_element_type=jnp.float32)
    imag = jnp.dot(whitened[:, bins:], order, preferred_element_type=jnp.float32)
    parts = (real[:, :half], imag[:, :half], real[:, half:], imag[:, half:])
    return [part.astype(jnp.bfloat16) for part in parts]


def whiten_kernel(spec_ref, out_ref):
    count, rows, width = spec_ref.shape
    half = width // 4
    parts = whiten(spec_ref[...].reshape(count * rows, width), bin_order(width // 2))
    for n, part in enumerate(parts):
        out_ref[:count, :, n * half : (n + 1) * half] = part.reshape(count, rows, half)
    out_ref[count] = jnp.zeros((rows, width), out_ref.dtype)


def greet(partners):
    barrier = pltpu.get_barrier_semaphore()
    for partner in partners:
        pl.semaphore_signal(
            barrier, inc=1, device_id=partner, device_id_type=pl.DeviceIdType.MESH
        )
    pl.semaphore_wait(barrier, len(partners))


def spread_kernel(
    size, lag_size, share, spec_ref, white_ref, held, order_ref, own_sem, send_sem, recv_sem,
):
    local_blocks, _, _, width = spec_ref.shape
    half = width // 4
    me = lax.axis_index("pair")
    lag = lax.axis_index("lag")

    chunk = local_blocks // CHUNKS if local_blocks % CHUNKS == 0 else local_blocks
    chunks = local_blocks // chunk

    def source(target, base, count):
        start = pl.multiple_of((target * lag_size + lag) * share, share)
        return spec_ref.at[base : base + count, 0, pl.ds(start, share), :]

    targets = [lax.rem(me + step, size) for step in range(1, size)]
    greet([{"pair": t} for t in targets])
    copies = {}
    for c in range(chunks):
        for n, target in enumerate(targets):
            copy = pltpu.make_async_remote_copy(
                src_ref=source(target, c * chunk, chunk),
                dst_ref=held.at[n + 1, c * chunk : (c + 1) * chunk],
                send_sem=send_sem.at[n * CHUNKS + c],
                recv_sem=recv_sem.at[n * CHUNKS + c],
                device_id={"pair": target},
                device_id_type=pl.DeviceIdType.MESH,
            )
            copy.start()
            copies[n + 1, c] = copy
    own = pltpu.make_async_copy(source(me, 0, local_blocks), held.at[0], own_sem)
    own.start()
    order_ref[...] = bin_order(width // 2)
    white_ref[local_blocks] = jnp.zeros(white_ref.shape[1:], white_ref.dtype)

    def finish(slot, base):
        origin = lax.rem(me - slot + size, size)
        values = held[slot, base : base + chunk].reshape(chunk * share, width)
        for n, part in enumerate(whiten(values, order_ref[...])):
            white_ref[base : base + chunk, origin, :, n * half : (n + 1) * half] = part.reshape(
                chunk, share, half
            )

    own.wait()
    for c in range(chunks):
        finish(0, c * chunk)
    for c in range(chunks):
        for step in sorted(range(1, size), key=lambda n: min(n, size - n)):
            copies[step, c].wait_recv()
            finish(step, c * chunk)
    for copy in copies.values():
        copy.wait_send()


def place_kernel(size, lag_size, share, piece, stack_ref, out_ref, own_sem, send_sem, recv_sem):
    me = lax.axis_index("pair") * lag_size + lax.axis_index("lag")
    rows = pl.ds(pl.multiple_of(me * share, share), share)

    def source(target):
        return stack_ref.at[:, :, pl.ds(pl.multiple_of(target * piece, piece), piece)]

    targets = [lax.rem(me + step, size) for step in range(1, size)]
    ids = [{"pair": lax.div(t, lag_size), "lag": lax.rem(t, lag_size)} for t in targets]
    greet(ids)
    copies = []
    for n, target in enumerate(targets):
        copy = pltpu.make_async_remote_copy(
            src_ref=source(target),
            dst_ref=out_ref.at[:, rows, :],
            send_sem=send_sem.at[n],
            recv_sem=recv_sem.at[n],
            device_id=ids[n],
            device_id_type=pl.DeviceIdType.MESH,
        )
        copy.start()
        copies.append(copy)
    own = pltpu.make_async_copy(source(me), out_ref.at[:, rows, :], own_sem)
    own.start()
    own.wait()
    for copy in copies:
        copy.wait()


def fused_kernel(
    size, lag_size, spec, pairs, live, groups, even_hbm, odd_hbm, out_ref,
    raw, send, whites, even_ref, odd_ref, order_ref, cross, prefix, stage, got,
    first_ids, second_ids, links, load_sem, table_sem, send_sem, recv_sem, give_sem, take_sem,
):
    local_blocks, _, _, width = spec.shape
    bins = width // 2
    half = bins // 2
    share = raw.shape[2]
    chunks = len(whites)
    devices = size * lag_size
    owners, slots = groups.shape
    quads = prefix.shape[1] - 1
    blank = whites[0].shape[0] - 1
    me = lax.axis_index("pair")
    lag = lax.axis_index("lag")
    place = me * lag_size + lag
    steps = [s for s in (2, 3, 1) if s < size] + [0]

    def device(step):
        return {
            "pair": lax.bitwise_xor(me, step // lag_size),
            "lag": lax.bitwise_xor(lag, step % lag_size),
        }

    barrier = pltpu.get_barrier_semaphore()
    for step in range(1, devices):
        pl.semaphore_signal(
            barrier, inc=1, device_id=device(step), device_id_type=pl.DeviceIdType.MESH
        )
    loads = []
    for n, step in enumerate(steps):
        target = lax.bitwise_xor(me, step)
        start = pl.multiple_of((target * lag_size + lag) * share, share)
        copy = pltpu.make_async_copy(
            spec.at[:, 0, pl.ds(start, share), :], raw.at[n], load_sem.at[n]
        )
        copy.start()
        loads.append(copy)
    fills = [
        pltpu.make_async_copy(even_hbm, even_ref, table_sem.at[0]),
        pltpu.make_async_copy(odd_hbm, odd_ref, table_sem.at[1]),
    ]
    for copy in fills:
        copy.start()
    order_ref[...] = bin_order(bins)

    low = lax.broadcasted_iota(jnp.int32, (local_blocks, 8, COLS), 1) < 4

    def swap(x):
        return pltpu.roll(x, 4, x.ndim - 2)

    def prepare(n):
        values = raw[n].reshape(local_blocks * share, width).astype(jnp.float32)
        power = jnp.sum(values * values, axis=-1, keepdims=True) * (1.0 / bins)
        whitened = (values * lax.rsqrt(power + EPSILON)).astype(jnp.bfloat16)
        for part in range(2):
            ordered = jnp.dot(
                whitened[:, part * bins : (part + 1) * bins], order_ref[...],
                preferred_element_type=jnp.float32,
            ).reshape(local_blocks, share, bins)
            for v in range(share // 8):
                tiles = [
                    ordered[:, 8 * v : 8 * v + 8, t * COLS : (t + 1) * COLS] for t in range(4)
                ]
                first = [jnp.where(low, tiles[2 * u], swap(tiles[2 * u + 1])) for u in range(2)]
                other = [jnp.where(low, swap(tiles[2 * u]), tiles[2 * u + 1]) for u in range(2)]
                for c, both in ((2 * v, first), (2 * v + 1, other)):
                    block = jnp.concatenate(both, axis=1).astype(jnp.bfloat16)
                    lanes = slice(part * COLS, (part + 1) * COLS)
                    if steps[n]:
                        send[c, n, :, :, lanes] = block
                    else:
                        whites[c][pl.ds(me * local_blocks, local_blocks), :, lanes] = block

    copies = {}

    def give(c, n):
        copy = pltpu.make_async_remote_copy(
            src_ref=send.at[c, n],
            dst_ref=whites[c].at[pl.ds(me * local_blocks, local_blocks)],
            send_sem=send_sem.at[c, n],
            recv_sem=recv_sem.at[c, n],
            device_id=device(steps[n] * lag_size),
            device_id_type=pl.DeviceIdType.MESH,
        )
        copy.start()
        copies[c, n] = copy

    for n in range(size):
        loads[n].wait()
        prepare(n)
        if n == 1:
            pl.semaphore_wait(barrier, devices - 1)
            give(0, 0)
            give(0, 1)
        if n == 2:
            give(0, 2)
            for c in range(1, chunks):
                for m in range(size - 1):
                    give(c, m)
    for white in whites:
        white[blank] = jnp.zeros(white.shape[1:], white.dtype)

    end = owners * slots

    def pick(g, values, default):
        for k in range(NGRP):
            default = jnp.where(g == k, values[k], default)
        return default

    def link_owner(p, carry):
        q = owners - 1 - p

        def link_slot(r, carry):
            heads, counts = carry
            s = slots - 1 - r
            g = groups[q, s]
            at = q * slots + s
            links[at] = pick(g, heads, end)
            used = s < live[q]
            hits = [jnp.logical_and(used, g == k) for k in range(NGRP)]
            heads = tuple(jnp.where(h, at, x) for h, x in zip(hits, heads))
            counts = tuple(jnp.where(h, x + 1, x) for h, x in zip(hits, counts))
            return heads, counts

        return lax.fori_loop(0, slots, link_slot, carry)

    zero = jnp.int32(0)
    last = jnp.int32(end)
    heads, counts = lax.fori_loop(0, owners, link_owner, ((last,) * NGRP, (zero,) * NGRP))
    links[end] = last

    def order_quad(n, carry):
        slot, group = carry
        for i in range(QUAD):
            stop = slot == end
            real = jnp.where(stop, 0, slot)
            q = real // slots
            s = real - q * slots

            def row(x):
                return jnp.where(stop, blank, (x % size) * local_blocks + x // size)

            first_ids[n * QUAD + i] = row(pairs[q, 0, s])
            second_ids[n * QUAD + i] = row(pairs[q, 1, s])
            slot = links[slot]
        done = slot == end
        group = jnp.where(done, group + 1, group)
        slot = jnp.where(done, pick(group, heads, last), slot)
        return slot, group

    lax.fori_loop(0, quads, order_quad, (heads[0], zero))
    ends = [zero]
    for k in range(NGRP):
        ends.append(ends[k] + (counts[k] + QUAD - 1) // QUAD)

    for n in range(3):
        prefix[n, 0] = jnp.zeros(prefix.shape[2:], prefix.dtype)
    for copy in fills:
        copy.wait()

    low8 = lax.broadcasted_iota(jnp.int32, (8, COLS), 0) < 4
    part_quads = quads // PARTS
    part_rows = part_quads * 16

    def fill_cross(white):
        def fill_quad(n, carry):
            products = []
            for i in range(QUAD):
                first = white[first_ids[n * QUAD + i]].astype(jnp.float32)
                second = white[second_ids[n * QUAD + i]].astype(jnp.float32)
                ra, ia = first[:, :COLS], first[:, COLS:]
                rb, ib = second[:, :COLS], second[:, COLS:]
                products.append((ra * rb + ia * ib, ia * rb - ra * ib))
            start = pl.multiple_of(n * 16, 16)
            for part in range(2):
                for h in range(2):
                    tops, bottoms = [], []
                    for i in range(0, QUAD, 2):
                        x = products[i][part][8 * h : 8 * h + 8]
                        y = products[i + 1][part][8 * h : 8 * h + 8]
                        tops.append(jnp.where(low8, x, swap(y)))
                        bottoms.append(jnp.where(low8, swap(x), y))
                    for j, tile in enumerate((tops, bottoms)):
                        at = (2 * part + j) * COLS
                        cross[h, pl.ds(start, 16), at : at + COLS] = jnp.concatenate(
                            tile, axis=0
                        ).astype(jnp.bfloat16)
            return carry

        lax.fori_loop(0, quads, fill_quad, 0)

    def add_part(p, carry):
        start = pl.multiple_of(p * part_rows, part_rows)
        base = p * part_quads
        for col in range(0, bins, COLS):
            def product(h, table):
                both = jnp.dot(
                    cross[h, pl.ds(start, part_rows), :],
                    table[:, 2 * col : 2 * (col + COLS)],
                    preferred_element_type=jnp.float32,
                )
                return both[:, :COLS], both[:, COLS:]

            even_d, even_q = product(0, even_ref)
            odd_d, odd_q = product(1, odd_ref)
            for side, at in ((-1, col), (1, bins + col)):
                sums = [prefix[n, base, :, at : at + COLS] for n in range(3)]
                for u in range(part_quads):
                    for i in range(2):
                        cut = slice(u * 16 + i * 8, u * 16 + i * 8 + 8)
                        if side < 0:
                            direct, quad = even_d[cut] - odd_d[cut], even_q[cut] - odd_q[cut]
                        else:
                            direct, quad = even_d[cut] + odd_d[cut], even_q[cut] + odd_q[cut]
                        inverse = jnp.minimum(
                            lax.rsqrt(direct * direct + quad * quad), 1.0 / AMP_FLOOR
                        )
                        terms = (direct, direct * inverse, quad * inverse)
                        sums = [x + y for x, y in zip(sums, terms)]
                    for n in range(3):
                        prefix[n, base + u + 1, :, at : at + COLS] = sums[n]
        return carry

    pad = 128
    lags = 2 * bins
    span = lags + pad
    piece = lags // devices
    low16 = lax.broadcasted_iota(jnp.int32, (8, lags), 0) < 4
    members = []
    for k in range(0, NGRP, 2):
        pair = [jnp.full((8, lags), counts[k + i].astype(jnp.float32)) for i in range(2)]
        members.append(jnp.where(low16, *pair))
    scale = 1.0 / jnp.sqrt(jnp.concatenate(members, axis=0))

    def stack(c):
        totals = []
        for n in range(3):
            rows = []
            for k in range(NGRP):
                total = prefix[n, ends[k + 1]] - prefix[n, ends[k]]
                rows.append(total + swap(total))
            totals.append(
                jnp.concatenate(
                    [jnp.where(low16, rows[k], rows[k + 1]) for k in range(0, NGRP, 2)], axis=0
                )
            )
        linear, cosine, sine = totals
        coherence = jnp.sqrt(cosine * cosine + sine * sine) * scale
        padded = jnp.concatenate([coherence, jnp.zeros((16, pad), jnp.float32)], axis=1)
        part, smooth, at = padded, padded, 1
        for n in range(1, 5):
            part = part + pltpu.roll(part, span - (1 << (n - 1)), 1)
            smooth = smooth + pltpu.roll(part, span - at, 1)
            at += 1 << n
        smooth = pltpu.roll(smooth, HW, 1)[:, :lags] * (1.0 / (2 * HW + 1))
        result = (linear * scale * smooth * smooth).astype(jnp.bfloat16)
        for t in range(devices):
            stage[c, t] = result[:, t * piece : (t + 1) * piece]
        got[c, place] = stage[c, place]
        for step in range(1, devices):
            target = device(step)
            copy = pltpu.make_async_remote_copy(
                src_ref=stage.at[c, target["pair"] * lag_size + target["lag"]],
                dst_ref=got.at[c, place],
                send_sem=give_sem.at[c, step - 1],
                recv_sem=take_sem.at[c, step - 1],
                device_id=target,
                device_id_type=pl.DeviceIdType.MESH,
            )
            copy.start()
            results[c, step] = copy

    low_out = lax.broadcasted_iota(jnp.int32, (devices, 8, piece), 1) < 4

    def assemble(v):
        for c in (2 * v, 2 * v + 1):
            for step in range(1, devices):
                results[c, step].wait_recv()
        a = got[2 * v].astype(jnp.float32)
        b = got[2 * v + 1].astype(jnp.float32)
        for k in range(0, NGRP, 2):
            x, y = a[:, 4 * k : 4 * k + 8], b[:, 4 * k : 4 * k + 8]
            out_ref[k, :, 8 * v : 8 * v + 8, :] = jnp.where(low_out, x, swap(y))
            out_ref[k + 1, :, 8 * v : 8 * v + 8, :] = jnp.where(low_out, swap(x), y)

    results = {}
    for c in range(chunks):
        for n in range(size - 1):
            copies[c, n].wait_recv()
        fill_cross(whites[c])
        lax.fori_loop(0, PARTS, add_part, 0)
        stack(c)
        if c >= 2 and c % 2 == 0:
            assemble(c // 2 - 1)
    assemble(chunks // 2 - 1)
    for copy in copies.values():
        copy.wait_send()
    for copy in results.values():
        copy.wait_send()


def fused(spectra, pairs, live, groups, even, odd, pair_size, lag_size, share):
    local_blocks, _, _, width = spectra.shape
    owners, slots = groups.shape
    blocks = local_blocks * pair_size
    devices = pair_size * lag_size
    chunks = share // CHUNK_ROWS
    quads = -(-(owners * slots // QUAD + NGRP) // PARTS) * PARTS
    piece = width // devices
    smem = pl.BlockSpec(memory_space=pltpu.SMEM)
    hbm = pl.BlockSpec(memory_space=pltpu.HBM)
    dma = pltpu.SemaphoreType.DMA
    out = pl.pallas_call(
        functools.partial(fused_kernel, pair_size, lag_size),
        out_shape=jax.ShapeDtypeStruct((NGRP, devices, share, piece), jnp.float32),
        in_specs=[hbm] + [smem] * 3 + [hbm] * 2,
        out_specs=pl.BlockSpec(memory_space=pltpu.VMEM),
        scratch_shapes=[
            pltpu.VMEM((pair_size, local_blocks, share, width), jnp.bfloat16),
            pltpu.VMEM((chunks, pair_size - 1, local_blocks, 16, 2 * COLS), jnp.bfloat16),
            [pltpu.VMEM((blocks + 1, 16, 2 * COLS), jnp.bfloat16)] * chunks,
            pltpu.VMEM(even.shape, jnp.bfloat16),
            pltpu.VMEM(odd.shape, jnp.bfloat16),
            pltpu.VMEM((width // 2, width // 2), jnp.bfloat16),
            pltpu.VMEM((2, quads * 16, width // 2), jnp.bfloat16),
            pltpu.VMEM((3, quads + 1, 8, width), jnp.float32),
            pltpu.VMEM((chunks, devices, 16, piece), jnp.bfloat16),
            pltpu.VMEM((chunks, devices, 16, piece), jnp.bfloat16),
            pltpu.SMEM((quads * QUAD,), jnp.int32),
            pltpu.SMEM((quads * QUAD,), jnp.int32),
            pltpu.SMEM((owners * slots + 1,), jnp.int32),
            dma((pair_size,)),
            dma((2,)),
            dma((chunks, pair_size - 1)),
            dma((chunks, pair_size - 1)),
            dma((chunks, devices - 1)),
            dma((chunks, devices - 1)),
        ],
        compiler_params=pltpu.CompilerParams(
            collective_id=2, has_side_effects=True, vmem_limit_bytes=50 << 20
        ),
    )(spectra, pairs, live, groups, even, odd)
    return out.reshape(NGRP, devices * share, piece)


def semaphores(count):
    return [
        pltpu.SemaphoreType.DMA,
        pltpu.SemaphoreType.DMA((count,)),
        pltpu.SemaphoreType.DMA((count,)),
    ]


def spread(spectra, pair_size, lag_size, share):
    local_blocks, _, _, width = spectra.shape
    blocks = local_blocks * pair_size
    vmem = pl.BlockSpec(memory_space=pltpu.VMEM)
    params = dict(vmem_limit_bytes=50 << 20)
    if share % ROWS:
        cells = spectra.reshape(local_blocks, pair_size, lag_size, share, width)
        cells = lax.dynamic_index_in_dim(cells, lax.axis_index("lag"), 2, keepdims=False)
        moved = lax.all_to_all(cells, "pair", 1, 1, tiled=True).reshape(blocks, share, width)
        rows = -(-share // ROWS) * ROWS
        return pl.pallas_call(
            whiten_kernel,
            out_shape=jax.ShapeDtypeStruct((blocks + 1, rows, width), jnp.bfloat16),
            in_specs=[vmem],
            out_specs=vmem,
            compiler_params=pltpu.CompilerParams(**params),
        )(jnp.pad(moved, ((0, 0), (0, rows - share), (0, 0))))
    white = pl.pallas_call(
        functools.partial(spread_kernel, pair_size, lag_size, share),
        out_shape=jax.ShapeDtypeStruct((local_blocks + 1, pair_size, share, width), jnp.bfloat16),
        in_specs=[pl.BlockSpec(memory_space=pltpu.HBM)],
        out_specs=vmem,
        scratch_shapes=[
            pltpu.VMEM((pair_size, local_blocks, share, width), spectra.dtype),
            pltpu.VMEM((width // 2, width // 2), jnp.bfloat16),
        ]
        + semaphores((pair_size - 1) * CHUNKS),
        compiler_params=pltpu.CompilerParams(collective_id=0, has_side_effects=True, **params),
    )(spectra)
    return white.reshape(blocks + pair_size, share, width)


def place(stacks, pair_size, lag_size, share):
    size = pair_size * lag_size
    groups, _, lags = stacks.shape
    piece = lags // size
    if share % ROWS or piece % 128:
        return lax.all_to_all(stacks[:, :share], ("pair", "lag"), 2, 1, tiled=True)
    return pl.pallas_call(
        functools.partial(place_kernel, size, lag_size, share, piece),
        out_shape=jax.ShapeDtypeStruct((groups, size * share, piece), stacks.dtype),
        in_specs=[pl.BlockSpec(memory_space=pl.ANY)],
        out_specs=pl.BlockSpec(memory_space=pltpu.VMEM),
        scratch_shapes=semaphores(size - 1),
        compiler_params=pltpu.CompilerParams(collective_id=1, has_side_effects=True),
    )(stacks)


def shards(spectra, pair_blocks, live_pairs, stack_group):
    pair_size = lax.axis_size("pair")
    lag_size = lax.axis_size("lag")
    _, _, channels, width = spectra.shape
    share = channels // (pair_size * lag_size)
    owners, slots = stack_group.shape
    even, odd = tables(width // 2)
    if share == ROWS and width == 8 * COLS and pair_size == 4 and lag_size == 2:
        pairs = pair_blocks.transpose(0, 2, 1)
        return fused(
            spectra, pairs, live_pairs, stack_group, even, odd, pair_size, lag_size, share
        )
    white = spread(spectra, pair_size, lag_size, share)
    rows = white.shape[1]
    smem = pl.BlockSpec(memory_space=pltpu.SMEM)
    vmem = pl.BlockSpec(memory_space=pltpu.VMEM)
    ids = pltpu.SMEM((NGRP * (owners * slots + QUAD) + QUAD,), jnp.int32)
    quads = pltpu.SMEM((owners * slots // QUAD + NGRP + BATCH,), jnp.int32)
    stacks = pl.pallas_call(
        kernel,
        out_shape=jax.ShapeDtypeStruct((NGRP, rows, width), jnp.bfloat16),
        in_specs=[smem] * 3 + [vmem] * 3,
        out_specs=vmem,
        scratch_shapes=[
            pltpu.VMEM((BATCH * rows, width), jnp.bfloat16),
            pltpu.VMEM((3, NGRP * rows, width), jnp.float32),
            ids, ids, quads, quads,
            pltpu.SMEM((NGRP,), jnp.int32),
        ],
        compiler_params=pltpu.CompilerParams(vmem_limit_bytes=40 << 20),
    )(
        pair_blocks.transpose(0, 2, 1), live_pairs, stack_group, white, even, odd
    )
    return place(stacks, pair_size, lag_size, share).astype(jnp.float32)


def solution(mesh):
    return jax.shard_map(
        shards,
        mesh=mesh,
        in_specs=(P("win", "pair", "stk", None), P("win", None, None), P("win"), P("win", None)),
        out_specs=P("win", "stk", ("pair", "lag")),
        check_vma=False,
    )
```

profile of v0, /device:TPU:0, one launch (start us, length us, event | category | flops | bytes accessed | tf_op | source)
XLA Modules:
  0.0 68.2 jit_solution(9124356531721938897)
XLA Ops:
  0.0 0.0 copy-start
  0.0 1.2 %copy-done = bf16[512,1024]{1,0:T(8,128)(2,1)S(1)} copy-done((bf16[512,1024]{1,0:T(8,128)(2,1)S(1)}, bf16[512,1024]{1,0:T(8,128)(2,1)}, u32[]{:S(2)}) %copy-start) | copy-done | bytes 1048600
  1.2 0.0 copy-start.1
  1.2 1.2 %copy-done.1 = bf16[512,1024]{1,0:T(8,128)(2,1)S(1)} copy-done((bf16[512,1024]{1,0:T(8,128)(2,1)S(1)}, bf16[512,1024]{1,0:T(8,128)(2,1)}, u32[]{:S(2)}) %copy-start.1) | copy-done | bytes 1048600
  2.5 0.0 copy-start.2
  2.5 0.7 %copy-done.2 = s32[4,40,2]{1,2,0:T(2,128)S(1)} copy-done((s32[4,40,2]{1,2,0:T(2,128)S(1)}, s32[4,40,2]{1,2,0:T(2,128)}, u32[]{:S(2)}) %copy-start.2) | copy-done | bytes 1304
  3.1 0.0 copy-start.3
  3.1 0.7 copy-done.3
  3.8 0.0 copy-start.4
  3.8 0.7 copy-done.4
  4.5 63.0 %shard_map.64 = f32[4,8,16,128]{3,2,1,0:T(8,128)S(1)} custom-call(bf16[16,1,128,1024]{3,2,1,0:T(8,128)(2,1)} %spec.1, s32[4,2,40]{2,1,0:T(2,128)S(1)} %bitcast.3, s32[4]{0:T(128)S(1)} %copy-done.4, s32[4,40]{1,0:T(4,128)S(1)} %copy-done.3, bf16[512,1024]{1,0:T(8,128)(2,1)S(1)} %copy-done.1, bf16[512,1024]{1,0:T(8,128)(2,1)S(1)} %copy-done), custom_call_target="tpu_custom_call" | custom-call | tf_op jit(solution)/shard_map/pallas_call | solution.py:586
  67.5 0.7 %copy.8 = f32[4,128,128]{2,1,0:T(8,128)} copy(f32[4,128,128]{2,1,0:T(8,128)S(1)} %bitcast.2) | data formatting | bytes 524288
Async XLA Ops:
  0.0 1.2 %copy-start = (bf16[512,1024]{1,0:T(8,128)(2,1)S(1)}, bf16[512,1024]{1,0:T(8,128)(2,1)}, u32[]{:S(2)}) copy-start(bf16[512,1024]{1,0:T(8,128)(2,1)} %constant.5.clone.odd_hbm) | copy-start | bytes 3145732
  1.2 1.2 %copy-start.1 = (bf16[512,1024]{1,0:T(8,128)(2,1)S(1)}, bf16[512,1024]{1,0:T(8,128)(2,1)}, u32[]{:S(2)}) copy-start(bf16[512,1024]{1,0:T(8,128)(2,1)} %constant.4.clone.even_hbm) | copy-start | bytes 3145732
  2.5 0.7 %copy-start.2 = (s32[4,40,2]{1,2,0:T(2,128)S(1)}, s32[4,40,2]{1,2,0:T(2,128)}, u32[]{:S(2)}) copy-start(s32[4,40,2]{1,2,0:T(2,128)} %param.7) | copy-start | bytes 3844
  3.1 0.7 copy-start.3
  3.8 0.7 copy-start.4
where the time goes:
time: 68.5 us; the launch traced here: 68.2 us
  Pallas kernels  63 us (92%)
  local copies, waits for them, and re-layouts  5.18 us (8%)
    pallas_call x1, Pallas kernels, fused(): pl.pallas_call(functools.partial(fused_kernel, pair_size, lag_size), out_...  63 us
    unnamed x11, local copies, waits for them, and re-layouts  5.18 us

commit v1 on v0

--- a/solution.py
+++ b/solution.py
@@ -270,9 +270,9 @@
 
 
 def fused_kernel(
-    size, lag_size, spec, pairs, live, groups, even_hbm, odd_hbm, out_ref,
+    size, lag_size, spec, pairs_hbm, live_hbm, groups_hbm, even_hbm, odd_hbm, out_ref,
     raw, send, whites, even_ref, odd_ref, order_ref, cross, prefix, stage, got,
-    first_ids, second_ids, links, load_sem, table_sem, send_sem, recv_sem, give_sem, take_sem,
+    pairs, live, groups, first_ids, second_ids, links, load_sem, table_sem, send_sem, recv_sem, give_sem, take_sem,
 ):
     local_blocks, _, _, width = spec.shape
     bins = width // 2
@@ -312,7 +312,12 @@
         pltpu.make_async_copy(even_hbm, even_ref, table_sem.at[0]),
         pltpu.make_async_copy(odd_hbm, odd_ref, table_sem.at[1]),
     ]
-    for copy in fills:
+    plans = [
+        pltpu.make_async_copy(pairs_hbm, pairs, table_sem.at[2]),
+        pltpu.make_async_copy(live_hbm, live, table_sem.at[3]),
+        pltpu.make_async_copy(groups_hbm, groups, table_sem.at[4]),
+    ]
+    for copy in plans + fills:
         copy.start()
     order_ref[...] = bin_order(bins)
 
@@ -374,6 +379,8 @@
         white[blank] = jnp.zeros(white.shape[1:], white.dtype)
 
     end = owners * slots
+    for copy in plans:
+        copy.wait()
 
     def pick(g, values, default):
         for k in range(NGRP):
@@ -580,13 +587,13 @@
     chunks = share // CHUNK_ROWS
     quads = -(-(owners * slots // QUAD + NGRP) // PARTS) * PARTS
     piece = width // devices
-    smem = pl.BlockSpec(memory_space=pltpu.SMEM)
+    operands = (spectra, pairs, live, groups, even, odd)
     hbm = pl.BlockSpec(memory_space=pltpu.HBM)
     dma = pltpu.SemaphoreType.DMA
     out = pl.pallas_call(
         functools.partial(fused_kernel, pair_size, lag_size),
         out_shape=jax.ShapeDtypeStruct((NGRP, devices, share, piece), jnp.float32),
-        in_specs=[hbm] + [smem] * 3 + [hbm] * 2,
+        in_specs=[hbm] * 6,
         out_specs=pl.BlockSpec(memory_space=pltpu.VMEM),
         scratch_shapes=[
             pltpu.VMEM((pair_size, local_blocks, share, width), jnp.bfloat16),
@@ -599,11 +606,14 @@
             pltpu.VMEM((3, quads + 1, 8, width), jnp.float32),
             pltpu.VMEM((chunks, devices, 16, piece), jnp.bfloat16),
             pltpu.VMEM((chunks, devices, 16, piece), jnp.bfloat16),
+            pltpu.SMEM(pairs.shape, jnp.int32),
+            pltpu.SMEM(live.shape, jnp.int32),
+            pltpu.SMEM(groups.shape, jnp.int32),
             pltpu.SMEM((quads * QUAD,), jnp.int32),
             pltpu.SMEM((quads * QUAD,), jnp.int32),
             pltpu.SMEM((owners * slots + 1,), jnp.int32),
             dma((pair_size,)),
-            dma((2,)),
+            dma((5,)),
             dma((chunks, pair_size - 1)),
             dma((chunks, pair_size - 1)),
             dma((chunks, devices - 1)),
@@ -612,7 +622,7 @@
         compiler_params=pltpu.CompilerParams(
             collective_id=2, has_side_effects=True, vmem_limit_bytes=50 << 20
         ),
-    )(spectra, pairs, live, groups, even, odd)
+    )(*(pltpu.with_memory_space_constraint(x, pltpu.HBM) for x in operands))
     return out.reshape(NGRP, devices * share, piece)
 
 

time: 68.5 us -> 63.2 us (0.923)
  local copies, waits for them, and re-layouts: 5.18 us -> 0.71 us
    unnamed x11 -> x1, local copies, waits for them, and re-layouts: 5.18 us -> 0.71 us
where the time goes in v1:
time: 63.2 us; the launch traced here: 63.1 us
  Pallas kernels  62.4 us (99%)
  local copies, waits for them, and re-layouts  0.71 us (1%)
    pallas_call x1, Pallas kernels, fused(): pl.pallas_call(functools.partial(fused_kernel, pair_size, lag_size), out_...  62.4 us

profile of v1, /device:TPU:0, one launch (start us, length us, event | category | flops | bytes accessed | tf_op | source)
XLA Modules:
  0.0 63.1 jit_solution(5147632124520943978)
XLA Ops:
  0.0 62.4 %shard_map.64 = f32[4,8,16,128]{3,2,1,0:T(8,128)S(1)} custom-call(bf16[16,1,128,1024]{3,2,1,0:T(8,128)(2,1)} %spec.1, s32[4,2,40]{2,1,0:T(2,128)} %bitcast.3, s32[4]{0:T(128)} %live_hbm.1, s32[4,40]{1,0:T(4,128)} %groups_hbm.1, bf16[512,1024]{1,0:T(8,128)(2,1)} %constant.4.clone.even_hbm, bf16[512,1024]{1,0:T(8,128)(2,1)} %constant.5.clone.odd_hbm), custom_call_target="tpu_custom_call" | custom-call | tf_op jit(solution)/shard_map/pallas_call | solution.py:593
  62.4 0.7 %copy.8 = f32[4,128,128]{2,1,0:T(8,128)} copy(f32[4,128,128]{2,1,0:T(8,128)S(1)} %bitcast.2) | data formatting | bytes 524288

commit v2 on v1

--- a/solution.py
+++ b/solution.py
@@ -535,29 +535,33 @@
         smooth = pltpu.roll(smooth, HW, 1)[:, :lags] * (1.0 / (2 * HW + 1))
         result = (linear * scale * smooth * smooth).astype(jnp.bfloat16)
         for t in range(devices):
-            stage[c, t] = result[:, t * piece : (t + 1) * piece]
-        got[c, place] = stage[c, place]
-        for step in range(1, devices):
+            stage[t, c] = result[:, t * piece : (t + 1) * piece]
+        got[place, c] = stage[place, c]
+
+    def give_results(turn, start, count):
+        for step in range(devices - 1, 0, -1):
             target = device(step)
+            cut = pl.ds(start, count)
             copy = pltpu.make_async_remote_copy(
-                src_ref=stage.at[c, target["pair"] * lag_size + target["lag"]],
-                dst_ref=got.at[c, place],
-                send_sem=give_sem.at[c, step - 1],
-                recv_sem=take_sem.at[c, step - 1],
+                src_ref=stage.at[target["pair"] * lag_size + target["lag"], cut],
+                dst_ref=got.at[place, cut],
+                send_sem=give_sem.at[turn, step - 1],
+                recv_sem=take_sem.at[turn, step - 1],
                 device_id=target,
                 device_id_type=pl.DeviceIdType.MESH,
             )
             copy.start()
-            results[c, step] = copy
+            results[turn, step] = copy
+
+    def take_results(turn):
+        for step in range(devices - 1, 0, -1):
+            results[turn, step].wait_recv()
 
     low_out = lax.broadcasted_iota(jnp.int32, (devices, 8, piece), 1) < 4
 
     def assemble(v):
-        for c in (2 * v, 2 * v + 1):
-            for step in range(1, devices):
-                results[c, step].wait_recv()
-        a = got[2 * v].astype(jnp.float32)
-        b = got[2 * v + 1].astype(jnp.float32)
+        a = got[:, 2 * v].astype(jnp.float32)
+        b = got[:, 2 * v + 1].astype(jnp.float32)
         for k in range(0, NGRP, 2):
             x, y = a[:, 4 * k : 4 * k + 8], b[:, 4 * k : 4 * k + 8]
             out_ref[k, :, 8 * v : 8 * v + 8, :] = jnp.where(low_out, x, swap(y))
@@ -567,11 +571,16 @@
     for c in range(chunks):
         for n in range(size - 1):
             copies[c, n].wait_recv()
+        if c == chunks - 1:
+            give_results(0, 0, c)
         fill_cross(whites[c])
         lax.fori_loop(0, PARTS, add_part, 0)
         stack(c)
-        if c >= 2 and c % 2 == 0:
-            assemble(c // 2 - 1)
+    give_results(1, chunks - 1, 1)
+    take_results(0)
+    for v in range(chunks // 2 - 1):
+        assemble(v)
+    take_results(1)
     assemble(chunks // 2 - 1)
     for copy in copies.values():
         copy.wait_send()
@@ -604,8 +613,8 @@
             pltpu.VMEM((width // 2, width // 2), jnp.bfloat16),
             pltpu.VMEM((2, quads * 16, width // 2), jnp.bfloat16),
             pltpu.VMEM((3, quads + 1, 8, width), jnp.float32),
-            pltpu.VMEM((chunks, devices, 16, piece), jnp.bfloat16),
-            pltpu.VMEM((chunks, devices, 16, piece), jnp.bfloat16),
+            pltpu.VMEM((devices, chunks, 16, piece), jnp.bfloat16),
+            pltpu.VMEM((devices, chunks, 16, piece), jnp.bfloat16),
             pltpu.SMEM(pairs.shape, jnp.int32),
             pltpu.SMEM(live.shape, jnp.int32),
             pltpu.SMEM(groups.shape, jnp.int32),
@@ -616,8 +625,8 @@
             dma((5,)),
             dma((chunks, pair_size - 1)),
             dma((chunks, pair_size - 1)),
-            dma((chunks, devices - 1)),
-            dma((chunks, devices - 1)),
+            dma((2, devices - 1)),
+            dma((2, devices - 1)),
         ],
         compiler_params=pltpu.CompilerParams(
             collective_id=2, has_side_effects=True, vmem_limit_bytes=50 << 20

time: 63.2 us -> 60.7 us (0.960)
  Pallas kernels: 62.4 us -> 59.8 us
    pallas_call x1, Pallas kernels: 62.4 us -> 59.8 us  [fused(): pl.pallas_call(functools.partial(fused_kernel, pair_size, lag_size), out_...]
where the time goes in v2:
time: 60.7 us; the launch traced here: 60.5 us
  Pallas kernels  59.8 us (99%)
  local copies, waits for them, and re-layouts  0.71 us (1%)
    pallas_call x1, Pallas kernels, fused(): pl.pallas_call(functools.partial(fused_kernel, pair_size, lag_size), out_...  59.8 us

profile of v2, /device:TPU:0, one launch (start us, length us, event | category | flops | bytes accessed | tf_op | source)
XLA Modules:
  0.0 60.5 jit_solution(16035080740206926401)
XLA Ops:
  0.0 59.8 %shard_map.64 = f32[4,8,16,128]{3,2,1,0:T(8,128)S(1)} custom-call(bf16[16,1,128,1024]{3,2,1,0:T(8,128)(2,1)} %spec.1, s32[4,2,40]{2,1,0:T(2,128)} %bitcast.3, s32[4]{0:T(128)} %live_hbm.1, s32[4,40]{1,0:T(4,128)} %groups_hbm.1, bf16[512,1024]{1,0:T(8,128)(2,1)} %constant.4.clone.even_hbm, bf16[512,1024]{1,0:T(8,128)(2,1)} %constant.5.clone.odd_hbm), custom_call_target="tpu_custom_call" | custom-call | tf_op jit(solution)/shard_map/pallas_call | solution.py:602
  59.8 0.7 %copy.8 = f32[4,128,128]{2,1,0:T(8,128)} copy(f32[4,128,128]{2,1,0:T(8,128)S(1)} %bitcast.2) | data formatting | bytes 524288

commit v3 on v2

--- a/solution.py
+++ b/solution.py
@@ -19,7 +19,7 @@
 CHUNKS = 4
 COLS = 128
 CHUNK_ROWS = 4
-PARTS = 2
+PARTS = 1
 
 
 def tables(num_bins):
@@ -273,6 +273,7 @@
     size, lag_size, spec, pairs_hbm, live_hbm, groups_hbm, even_hbm, odd_hbm, out_ref,
     raw, send, whites, even_ref, odd_ref, order_ref, cross, prefix, stage, got,
     pairs, live, groups, first_ids, second_ids, links, load_sem, table_sem, send_sem, recv_sem, give_sem, take_sem,
+    far_sem, side_sem,
 ):
     local_blocks, _, _, width = spec.shape
     bins = width // 2
@@ -286,7 +287,8 @@
     me = lax.axis_index("pair")
     lag = lax.axis_index("lag")
     place = me * lag_size + lag
-    steps = [s for s in (2, 3, 1) if s < size] + [0]
+    steps = [3, 2, 1, 0]
+    middle = jnp.logical_or(me == 1, me == 2)
 
     def device(step):
         return {
@@ -294,11 +296,19 @@
             "lag": lax.bitwise_xor(lag, step % lag_size),
         }
 
+    def signal(sem, step):
+        pl.semaphore_signal(
+            sem, inc=1, device_id=device(step), device_id_type=pl.DeviceIdType.MESH
+        )
+
     barrier = pltpu.get_barrier_semaphore()
-    for step in range(1, devices):
-        pl.semaphore_signal(
-            barrier, inc=1, device_id=device(step), device_id_type=pl.DeviceIdType.MESH
-        )
+    signal(barrier, 1)
+    signal(barrier, lag_size)
+
+    @pl.when(middle)
+    def _():
+        signal(barrier, 3 * lag_size)
+
     loads = []
     for n, step in enumerate(steps):
         target = lax.bitwise_xor(me, step)
@@ -352,7 +362,7 @@
     copies = {}
 
     def give(c, n):
-        copy = pltpu.make_async_remote_copy(
+        return pltpu.make_async_remote_copy(
             src_ref=send.at[c, n],
             dst_ref=whites[c].at[pl.ds(me * local_blocks, local_blocks)],
             send_sem=send_sem.at[c, n],
@@ -360,21 +370,46 @@
             device_id=device(steps[n] * lag_size),
             device_id_type=pl.DeviceIdType.MESH,
         )
-        copy.start()
-        copies[c, n] = copy
-
-    for n in range(size):
-        loads[n].wait()
-        prepare(n)
-        if n == 1:
-            pl.semaphore_wait(barrier, devices - 1)
-            give(0, 0)
-            give(0, 1)
-        if n == 2:
-            give(0, 2)
-            for c in range(1, chunks):
-                for m in range(size - 1):
-                    give(c, m)
+
+    for c in range(chunks):
+        for n in range(size - 1):
+            copies[c, n] = give(c, n)
+    loads[0].wait()
+    prepare(0)
+
+    @pl.when(middle)
+    def _():
+        pl.semaphore_wait(barrier, 3)
+        signal(far_sem, 3 * lag_size)
+        signal(far_sem, lag_size)
+        copies[0, 0].start()
+
+    loads[1].wait()
+    prepare(1)
+
+    @pl.when(middle)
+    def _():
+        pl.semaphore_wait(far_sem, 1)
+        signal(far_sem, lag_size)
+        copies[0, 1].start()
+
+    @pl.when(jnp.logical_not(middle))
+    def _():
+        pl.semaphore_wait(barrier, 2)
+        pl.semaphore_wait(far_sem, 1)
+        copies[0, 1].start()
+        pl.semaphore_wait(far_sem, 1)
+        copies[0, 0].start()
+
+    signal(side_sem, 1)
+    loads[2].wait()
+    prepare(2)
+    copies[0, 2].start()
+    for c in range(1, chunks):
+        for n in (1, 0, 2):
+            copies[c, n].start()
+    loads[3].wait()
+    prepare(3)
     for white in whites:
         white[blank] = jnp.zeros(white.shape[1:], white.dtype)
 
@@ -467,7 +502,7 @@
                         ).astype(jnp.bfloat16)
             return carry
 
-        lax.fori_loop(0, quads, fill_quad, 0)
+        lax.fori_loop(0, quads, fill_quad, 0, unroll=2)
 
     def add_part(p, carry):
         start = pl.multiple_of(p * part_rows, part_rows)
@@ -527,12 +562,10 @@
         linear, cosine, sine = totals
         coherence = jnp.sqrt(cosine * cosine + sine * sine) * scale
         padded = jnp.concatenate([coherence, jnp.zeros((16, pad), jnp.float32)], axis=1)
-        part, smooth, at = padded, padded, 1
-        for n in range(1, 5):
-            part = part + pltpu.roll(part, span - (1 << (n - 1)), 1)
-            smooth = smooth + pltpu.roll(part, span - at, 1)
-            at += 1 << n
-        smooth = pltpu.roll(smooth, HW, 1)[:, :lags] * (1.0 / (2 * HW + 1))
+        part = padded
+        for n in range(4):
+            part = part + pltpu.roll(part, 1 << n, 1)
+        smooth = (part + pltpu.roll(part, span - HW, 1) - padded)[:, :lags] * (1.0 / (2 * HW + 1))
         result = (linear * scale * smooth * smooth).astype(jnp.bfloat16)
         for t in range(devices):
             stage[t, c] = result[:, t * piece : (t + 1) * piece]
@@ -572,6 +605,7 @@
         for n in range(size - 1):
             copies[c, n].wait_recv()
         if c == chunks - 1:
+            pl.semaphore_wait(side_sem, 1)
             give_results(0, 0, c)
         fill_cross(whites[c])
         lax.fori_loop(0, PARTS, add_part, 0)
@@ -627,6 +661,8 @@
             dma((chunks, pair_size - 1)),
             dma((2, devices - 1)),
             dma((2, devices - 1)),
+            pltpu.SemaphoreType.REGULAR,
+            pltpu.SemaphoreType.REGULAR,
         ],
         compiler_params=pltpu.CompilerParams(
             collective_id=2, has_side_effects=True, vmem_limit_bytes=50 << 20

time: 60.7 us -> 59 us (0.972)
  Pallas kernels: 59.8 us -> 58.2 us
    pallas_call x1, Pallas kernels: 59.8 us -> 58.2 us  [fused(): pl.pallas_call(functools.partial(fused_kernel, pair_size, lag_size), out_...]
where the time goes in v3:
time: 59 us; the launch traced here: 58.9 us
  Pallas kernels  58.2 us (99%)
  local copies, waits for them, and re-layouts  0.71 us (1%)
    pallas_call x1, Pallas kernels, fused(): pl.pallas_call(functools.partial(fused_kernel, pair_size, lag_size), out_...  58.2 us

profile of v3, /device:TPU:0, one launch (start us, length us, event | category | flops | bytes accessed | tf_op | source)
XLA Modules:
  0.0 58.9 jit_solution(5968236980267916163)
XLA Ops:
  0.0 58.2 %shard_map.64 = f32[4,8,16,128]{3,2,1,0:T(8,128)S(1)} custom-call(bf16[16,1,128,1024]{3,2,1,0:T(8,128)(2,1)} %spec.1, s32[4,2,40]{2,1,0:T(2,128)} %bitcast.3, s32[4]{0:T(128)} %live_hbm.1, s32[4,40]{1,0:T(4,128)} %groups_hbm.1, bf16[512,1024]{1,0:T(8,128)(2,1)} %constant.4.clone.even_hbm, bf16[512,1024]{1,0:T(8,128)(2,1)} %constant.5.clone.odd_hbm), custom_call_target="tpu_custom_call" | custom-call | tf_op jit(solution)/shard_map/pallas_call | solution.py:636
  58.2 0.7 %copy.8 = f32[4,128,128]{2,1,0:T(8,128)} copy(f32[4,128,128]{2,1,0:T(8,128)S(1)} %bitcast.2) | data formatting | bytes 524288

commit v4 on v3

--- a/solution.py
+++ b/solution.py
@@ -571,8 +571,8 @@
             stage[t, c] = result[:, t * piece : (t + 1) * piece]
         got[place, c] = stage[place, c]
 
-    def give_results(turn, start, count):
-        for step in range(devices - 1, 0, -1):
+    def give_results(turn, start, count, order=(5, 4, 7, 6, 3, 2, 1)):
+        for step in order:
             target = device(step)
             cut = pl.ds(start, count)
             copy = pltpu.make_async_remote_copy(
@@ -604,12 +604,14 @@
     for c in range(chunks):
         for n in range(size - 1):
             copies[c, n].wait_recv()
+        fill_cross(whites[c])
         if c == chunks - 1:
-            pl.semaphore_wait(side_sem, 1)
-            give_results(0, 0, c)
-        fill_cross(whites[c])
+            give_results(0, 0, c, (5, 4, 7, 6))
         lax.fori_loop(0, PARTS, add_part, 0)
         stack(c)
+        if c == chunks - 2:
+            pl.semaphore_wait(side_sem, 1)
+            give_results(0, 0, chunks - 1, (3, 2, 1))
     give_results(1, chunks - 1, 1)
     take_results(0)
     for v in range(chunks // 2 - 1):

time: 59 us -> 59 us (level)
  no operation moved by 1% of the time
where the time goes in v4:
time: 59 us; the launch traced here: 58.9 us
  Pallas kernels  58.2 us (99%)
  local copies, waits for them, and re-layouts  0.71 us (1%)
    pallas_call x1, Pallas kernels, fused(): pl.pallas_call(functools.partial(fused_kernel, pair_size, lag_size), out_...  58.2 us

profile of v4, /device:TPU:0, one launch (start us, length us, event | category | flops | bytes accessed | tf_op | source)
XLA Modules:
  0.0 58.9 jit_solution(5223831582545591465)
XLA Ops:
  0.0 58.2 %shard_map.64 = f32[4,8,16,128]{3,2,1,0:T(8,128)S(1)} custom-call(bf16[16,1,128,1024]{3,2,1,0:T(8,128)(2,1)} %spec.1, s32[4,2,40]{2,1,0:T(2,128)} %bitcast.3, s32[4]{0:T(128)} %live_hbm.1, s32[4,40]{1,0:T(4,128)} %groups_hbm.1, bf16[512,1024]{1,0:T(8,128)(2,1)} %constant.4.clone.even_hbm, bf16[512,1024]{1,0:T(8,128)(2,1)} %constant.5.clone.odd_hbm), custom_call_target="tpu_custom_call" | custom-call | tf_op jit(solution)/shard_map/pallas_call | solution.py:638
  58.2 0.7 %copy.8 = f32[4,128,128]{2,1,0:T(8,128)} copy(f32[4,128,128]{2,1,0:T(8,128)S(1)} %bitcast.2) | data formatting | bytes 524288
